TPU v7x, 32 devices: a whole 2x2x4 slice. The times are simulated.
32 devices in a mesh: section: 2 (over x), dp: 16 (over z, y, core).
Axes of the slice: x: 2, y: 2, z: 4, core: 2. Of those that a mesh axis runs over, the one named last changes fastest.
Arguments:
- stream_in: bfloat16 [128, 8192], P(None, 'dp'), may hold values from -6 to 6
- gains: float32 [2, 8192], P('section'), may hold values from 0.5 to 1.5
- weights: bfloat16 [2, 8192, 8192], P('section', 'dp'), may hold values from -6 to 6
- masks: int32 [2, 8192, 128], P('section', 'dp'), may hold values 0 or 1
- inv_hessian: float32 [2, 64, 128, 128], P('section', 'dp'), may hold values from -0.025 to 3.2
Outputs:
- stream_out: bfloat16 [2, 128, 8192], P('section', None, 'dp')
- refitted: bfloat16 [2, 8192, 8192], P('section', 'dp')
All inputs are finite; a program needn't handle non-finite values. No bound on the sum of `masks` on one device may be relied on, other than what follows from the above.
Results may differ from a plain program's by a relative error of at most 0.015.
Values may be sent and summed in bfloat16 or wider, within the bound.
A program may use at most 128 MiB of HBM per device.

v0:
```python
import jax
import jax.numpy as jnp
from jax import lax
from jax.sharding import PartitionSpec as P

D = 8192
BLOCK = 128


def passed_along(value, axis, steps):
    count = lax.axis_size(axis)
    first, last = (max(0, -steps), min(count, count - steps))
    return lax.ppermute(value, axis, [(source, source + steps) for source in range(first, last)])


def body(stream_in, gains, weights, masks, inv_hessian):
    section_index = lax.axis_index("section")
    dp_index = lax.axis_index("dp")
    owned_cols = stream_in.shape[1]
    keep = jnp.repeat(masks[0], BLOCK // 2, axis=1)
    kept_rows = weights[0] * keep.astype(jnp.bfloat16)
    gain_row = gains[0]
    tok_count = stream_in.shape[0]
    micro_count = 4
    micro_rows = tok_count // micro_count
    step_count = lax.axis_size("section") + micro_count - 1
    scale = D ** (-0.5)
    inverse_whole = inv_hessian[0]

    def advance(moment, state):
        outgoing, normed_store, produced = state
        received = passed_along(outgoing, "section", 1)
        micro_index = moment - section_index
        active = (micro_index >= 0) & (micro_index < micro_count)
        offset = jnp.clip(micro_index, 0, micro_count - 1) * micro_rows
        x_rows = lax.dynamic_slice_in_dim(stream_in, offset, micro_rows, 0)
        window = jnp.where(section_index == 0, x_rows, received)
        widened = lax.all_gather(window, "dp", axis=1, tiled=True).astype(jnp.float32)
        mean_square = jnp.mean(widened * widened, axis=1, keepdims=True)
        normed = (widened * lax.rsqrt(mean_square + 1e-05) * gain_row).astype(jnp.bfloat16)
        projected = (
            lax.dot_general(
                normed, kept_rows, (((1,), (1,)), ((), ())), preferred_element_type=jnp.float32
            )
            * scale
        )
        new_window = (window.astype(jnp.float32) + projected).astype(jnp.bfloat16)
        stored = lax.dynamic_slice_in_dim(normed, dp_index * owned_cols, owned_cols, 1)
        prior_normed = lax.dynamic_slice_in_dim(normed_store, offset, micro_rows, 0)
        normed_store = lax.dynamic_update_slice_in_dim(
            normed_store, jnp.where(active, stored, prior_normed), offset, 0
        )
        prior_out = lax.dynamic_slice_in_dim(produced, offset, micro_rows, 0)
        produced = lax.dynamic_update_slice_in_dim(
            produced, jnp.where(active, new_window, prior_out), offset, 0
        )
        return (new_window, normed_store, produced)

    start_state = (
        jnp.zeros((micro_rows, owned_cols), jnp.bfloat16),
        jnp.zeros((tok_count, owned_cols), jnp.bfloat16),
        jnp.zeros((tok_count, owned_cols), jnp.bfloat16),
    )
    outgoing, normed_store, produced = lax.fori_loop(0, step_count, advance, start_state)
    blocks = normed_store.reshape(tok_count, -1, BLOCK)
    gram_local = jnp.einsum("tbi,tbj->bij", blocks, blocks, preferred_element_type=jnp.float32)
    out_rows = weights.shape[1]
    removed = weights[0].astype(jnp.float32) * (1 - keep).astype(jnp.float32)
    removed = removed.reshape(out_rows, -1, BLOCK)
    hessian_local = gram_local * (1.0 / tok_count)
    hessian, inverse = (
        lax.all_gather(hessian_local.astype(jnp.bfloat16), "dp", axis=0, tiled=True).astype(
            hessian_local.dtype
        ),
        lax.all_gather(inverse_whole.astype(jnp.bfloat16), "dp", axis=0, tiled=True).astype(
            inverse_whole.dtype
        ),
    )
    gradient = jnp.einsum("rbi,bij->rbj", removed, hessian, precision=lax.Precision.HIGHEST)
    update_step = jnp.einsum("rbi,bij->rbj", gradient, inverse, precision=lax.Precision.HIGHEST)
    refitted = keep.astype(jnp.float32) * (
        weights[0].astype(jnp.float32) + update_step.reshape(out_rows, -1)
    )
    return (produced[None], refitted.astype(jnp.bfloat16)[None])


def solution(mesh):
    placed = (
        P(None, "dp"),
        P("section", None),
        P("section", "dp", None),
        P("section", "dp", None),
        P("section", "dp", None, None),
    )
    return jax.shard_map(
        body,
        mesh=mesh,
        in_specs=placed,
        out_specs=(P("section", None, "dp"), P("section", "dp", None)),
        check_vma=False,
    )
```

profile of v0, /device:TPU:0, one launch (start us, length us, event | category | flops | bytes accessed | tf_op | source)
XLA Modules:
  0.0 337.2 jit_solution(13936854708661904504)
XLA Ops:
  7.2 0.0 all-gather.4.cloned.1.call-start
  7.2 0.0 copy-start.2
  7.2 12.0 %copy.17 = bf16[1,512,8192]{1,2,0:T(8,128)(2,1)} copy(bf16[1,512,8192]{2,1,0:T(8,128)(2,1)} %param.9) | data formatting | bytes 16777216 | tf_op args[2]
  19.2 0.0 copy-done.2
  19.2 0.1 convert_bitcast_fusion.1
  19.3 0.1 copy.18
  19.4 7.2 %bitcast_multiply_fusion.1 = bf16[512,8192]{0,1:T(8,128)(2,1)} fusion(bf16[1,512,8192]{1,2,0:T(8,128)(2,1)} %copy.17, bf16[512,128]{0,1:T(8,128)(2,1)S(1)} %copy.18), kind=kLoop, calls=%fused_computation.18 | loop fusion | flops 4194304 | bytes 16908288 | tf_op jit(solution)/shard_map/mul | solution.py:21
  26.6 12.0 %copy.19 = bf16[512,8192]{1,0:T(8,128)(2,1)} copy(bf16[512,8192]{0,1:T(8,128)(2,1)} %bitcast_multiply_fusion.1) | data formatting | bytes 16777216
  38.6 0.0 copy-done
  38.6 0.0 copy-start.3
  38.6 167.6 %while.20 = (s32[]{:T(128)}, bf16[32,512]{1,0:T(8,128)(2,1)S(1)}, bf16[128,512]{1,0:T(8,128)(2,1)S(1)}, bf16[128,512]{1,0:T(8,128)(2,1)S(1)}, pred[]{:T(512)}, /...) while((s32[]{:T(128)}, bf16[32,512]{1,0:T(8,128)(2,1)S(1)}, ...), condition=%wide.region_2.3_spmd.clone, body=%wide.region_0.2_spmd.clone.sunk | while | flops 270401568 | bytes 11600705 | solution.py:64
  38.6 5.0 %collective-permute-start = (bf16[32,512]{1,0:T(8,128)(2,1)S(1)}, bf16[32,512]{1,0:T(8,128)(2,1)S(1)}, u32[]{:S(2)}, u32[]{:S(2)}) collective-permute-start(bf16[32,512]{1,0:T(8,128)(2,1)S(1)} %broadcast_select_fusion.2), channel_id=1, source_target_pairs={{0,16},{1,17},{2,18},{3,19},{4,20},{5,21},{6,22},{7,23},{8,24},{9,... | collective-permute-start | bytes 98312 | tf_op jit(solution)/shard_map/while/body/eval_jaxpr/ppermute | solution.py:13
  43.6 1.6 collective-permute-done
  45.2 0.8 dynamic-slice_select_fusion.2
  46.0 23.2 %all_gather.19 = bf16[32,8192]{1,0:T(8,128)(2,1)S(1)} all-gather(bf16[32,512]{1,0:T(8,128)(2,1)S(1)} %dynamic-slice_select_fusion.2), channel_id=1, replica_groups=mesh['section'=2,'dp'=16] {'dp'}, dimensions={1}, use_global_device_ids=true | all-gather | bytes 557056 | tf_op jit(solution)/shard_map/while/body/eval_jaxpr/all_gather | solution.py:38
  69.2 0.2 fusion.23
  69.5 0.2 fusion.24
  69.7 6.0 %select_dynamic-update-slice_fusion.4 = (bf16[128,512]{1,0:T(8,128)(2,1)S(1)}, bf16[32,512]{1,0:T(8,128)(2,1)S(1)}) fusion(bf16[128,512]{1,0:T(8,128)(2,1)S(1)} %get-tuple-element.392, s32[]{:T(128)S(6)} %select_n.96, pred[]{:T(512)S(6)} %and.13, bf16[32,8192]{1,0:T(8,128)(2,1)S(1)} %fusion.24, bf16[512,8192]{1,0:T(8,128)(2,1)} %get-tuple-element.413, ...), kind=kOutput, calls=%fused_computation.7.clone.1 | convolution fusion | flops 268517376 | bytes 9043973 | tf_op jit(solution)/shard_map/while/body/eval_jaxpr/dot_general | solution.py:42
  75.7 4.2 %collective-permute-start = (bf16[32,512]{1,0:T(8,128)(2,1)S(1)}, bf16[32,512]{1,0:T(8,128)(2,1)S(1)}, u32[]{:S(2)}, u32[]{:S(2)}) collective-permute-start(bf16[32,512]{1,0:T(8,128)(2,1)S(1)} %broadcast_select_fusion.2), channel_id=1, source_target_pairs={{0,16},{1,17},{2,18},{3,19},{4,20},{5,21},{6,22},{7,23},{8,24},{9,... | collective-permute-start | bytes 98312 | tf_op jit(solution)/shard_map/while/body/eval_jaxpr/ppermute | solution.py:13
  80.0 1.6 collective-permute-done
  81.5 0.8 dynamic-slice_select_fusion.2
  82.3 18.8 %all_gather.19 = bf16[32,8192]{1,0:T(8,128)(2,1)S(1)} all-gather(bf16[32,512]{1,0:T(8,128)(2,1)S(1)} %dynamic-slice_select_fusion.2), channel_id=1, replica_groups=mesh['section'=2,'dp'=16] {'dp'}, dimensions={1}, use_global_device_ids=true | all-gather | bytes 557056 | tf_op jit(solution)/shard_map/while/body/eval_jaxpr/all_gather | solution.py:38
  101.1 0.2 fusion.23
  101.3 0.2 fusion.24
  101.5 6.0 %select_dynamic-update-slice_fusion.4 = (bf16[128,512]{1,0:T(8,128)(2,1)S(1)}, bf16[32,512]{1,0:T(8,128)(2,1)S(1)}) fusion(bf16[128,512]{1,0:T(8,128)(2,1)S(1)} %get-tuple-element.392, s32[]{:T(128)S(6)} %select_n.96, pred[]{:T(512)S(6)} %and.13, bf16[32,8192]{1,0:T(8,128)(2,1)S(1)} %fusion.24, bf16[512,8192]{1,0:T(8,128)(2,1)} %get-tuple-element.413, ...), kind=kOutput, calls=%fused_computation.7.clone.1 | convolution fusion | flops 268517376 | bytes 9043973 | tf_op jit(solution)/shard_map/while/body/eval_jaxpr/dot_general | solution.py:42
  107.5 4.2 %collective-permute-start = (bf16[32,512]{1,0:T(8,128)(2,1)S(1)}, bf16[32,512]{1,0:T(8,128)(2,1)S(1)}, u32[]{:S(2)}, u32[]{:S(2)}) collective-permute-start(bf16[32,512]{1,0:T(8,128)(2,1)S(1)} %broadcast_select_fusion.2), channel_id=1, source_target_pairs={{0,16},{1,17},{2,18},{3,19},{4,20},{5,21},{6,22},{7,23},{8,24},{9,... | collective-permute-start | bytes 98312 | tf_op jit(solution)/shard_map/while/body/eval_jaxpr/ppermute | solution.py:13
  111.7 1.6 collective-permute-done
  113.3 0.8 dynamic-slice_select_fusion.2
  114.1 20.5 %all_gather.19 = bf16[32,8192]{1,0:T(8,128)(2,1)S(1)} all-gather(bf16[32,512]{1,0:T(8,128)(2,1)S(1)} %dynamic-slice_select_fusion.2), channel_id=1, replica_groups=mesh['section'=2,'dp'=16] {'dp'}, dimensions={1}, use_global_device_ids=true | all-gather | bytes 557056 | tf_op jit(solution)/shard_map/while/body/eval_jaxpr/all_gather | solution.py:38
  134.5 0.2 fusion.23
  134.8 0.2 fusion.24
  135.0 6.0 %select_dynamic-update-slice_fusion.4 = (bf16[128,512]{1,0:T(8,128)(2,1)S(1)}, bf16[32,512]{1,0:T(8,128)(2,1)S(1)}) fusion(bf16[128,512]{1,0:T(8,128)(2,1)S(1)} %get-tuple-element.392, s32[]{:T(128)S(6)} %select_n.96, pred[]{:T(512)S(6)} %and.13, bf16[32,8192]{1,0:T(8,128)(2,1)S(1)} %fusion.24, bf16[512,8192]{1,0:T(8,128)(2,1)} %get-tuple-element.413, ...), kind=kOutput, calls=%fused_computation.7.clone.1 | convolution fusion | flops 268517376 | bytes 9043973 | tf_op jit(solution)/shard_map/while/body/eval_jaxpr/dot_general | solution.py:42
  141.0 4.1 %collective-permute-start = (bf16[32,512]{1,0:T(8,128)(2,1)S(1)}, bf16[32,512]{1,0:T(8,128)(2,1)S(1)}, u32[]{:S(2)}, u32[]{:S(2)}) collective-permute-start(bf16[32,512]{1,0:T(8,128)(2,1)S(1)} %broadcast_select_fusion.2), channel_id=1, source_target_pairs={{0,16},{1,17},{2,18},{3,19},{4,20},{5,21},{6,22},{7,23},{8,24},{9,... | collective-permute-start | bytes 98312 | tf_op jit(solution)/shard_map/while/body/eval_jaxpr/ppermute | solution.py:13
  145.2 1.6 collective-permute-done
  146.8 0.8 dynamic-slice_select_fusion.2
  147.5 18.7 %all_gather.19 = bf16[32,8192]{1,0:T(8,128)(2,1)S(1)} all-gather(bf16[32,512]{1,0:T(8,128)(2,1)S(1)} %dynamic-slice_select_fusion.2), channel_id=1, replica_groups=mesh['section'=2,'dp'=16] {'dp'}, dimensions={1}, use_global_device_ids=true | all-gather | bytes 557056 | tf_op jit(solution)/shard_map/while/body/eval_jaxpr/all_gather | solution.py:38
  166.3 0.2 fusion.23
  166.5 0.2 fusion.24
  166.7 6.0 %select_dynamic-update-slice_fusion.4 = (bf16[128,512]{1,0:T(8,128)(2,1)S(1)}, bf16[32,512]{1,0:T(8,128)(2,1)S(1)}) fusion(bf16[128,512]{1,0:T(8,128)(2,1)S(1)} %get-tuple-element.392, s32[]{:T(128)S(6)} %select_n.96, pred[]{:T(512)S(6)} %and.13, bf16[32,8192]{1,0:T(8,128)(2,1)S(1)} %fusion.24, bf16[512,8192]{1,0:T(8,128)(2,1)} %get-tuple-element.413, ...), kind=kOutput, calls=%fused_computation.7.clone.1 | convolution fusion | flops 268517376 | bytes 9043973 | tf_op jit(solution)/shard_map/while/body/eval_jaxpr/dot_general | solution.py:42
  172.8 4.2 %collective-permute-start = (bf16[32,512]{1,0:T(8,128)(2,1)S(1)}, bf16[32,512]{1,0:T(8,128)(2,1)S(1)}, u32[]{:S(2)}, u32[]{:S(2)}) collective-permute-start(bf16[32,512]{1,0:T(8,128)(2,1)S(1)} %broadcast_select_fusion.2), channel_id=1, source_target_pairs={{0,16},{1,17},{2,18},{3,19},{4,20},{5,21},{6,22},{7,23},{8,24},{9,... | collective-permute-start | bytes 98312 | tf_op jit(solution)/shard_map/while/body/eval_jaxpr/ppermute | solution.py:13
  177.0 1.6 collective-permute-done
  178.5 0.8 dynamic-slice_select_fusion.2
  179.3 20.5 %all_gather.19 = bf16[32,8192]{1,0:T(8,128)(2,1)S(1)} all-gather(bf16[32,512]{1,0:T(8,128)(2,1)S(1)} %dynamic-slice_select_fusion.2), channel_id=1, replica_groups=mesh['section'=2,'dp'=16] {'dp'}, dimensions={1}, use_global_device_ids=true | all-gather | bytes 557056 | tf_op jit(solution)/shard_map/while/body/eval_jaxpr/all_gather | solution.py:38
  199.8 0.2 fusion.23
  200.0 0.2 fusion.24
  200.2 6.0 %select_dynamic-update-slice_fusion.4 = (bf16[128,512]{1,0:T(8,128)(2,1)S(1)}, bf16[32,512]{1,0:T(8,128)(2,1)S(1)}) fusion(bf16[128,512]{1,0:T(8,128)(2,1)S(1)} %get-tuple-element.392, s32[]{:T(128)S(6)} %select_n.96, pred[]{:T(512)S(6)} %and.13, bf16[32,8192]{1,0:T(8,128)(2,1)S(1)} %fusion.24, bf16[512,8192]{1,0:T(8,128)(2,1)} %get-tuple-element.413, ...), kind=kOutput, calls=%fused_computation.7.clone.1 | convolution fusion | flops 268517376 | bytes 9043973 | tf_op jit(solution)/shard_map/while/body/eval_jaxpr/dot_general | solution.py:42
  206.2 0.0 copy-start.1
  206.2 0.9 fusion.8
  207.1 0.0 all-gather.4.cloned.1.call-update
  207.1 0.0 all-gather.6.cloned.1.call-start
  207.2 0.0 copy-done.3
  207.2 0.7 bitcast_convert_fusion
  207.9 0.0 all-gather.6.cloned.1.call-update
  207.9 0.1 copy.20
  208.0 0.1 copy.24
  208.2 2.1 broadcast_in_dim.21
  210.3 0.0 copy-done.1
  210.3 10.5 %bitcast_multiply_fusion = f32[512,64,128]{0,2,1:T(8,128)} fusion(bf16[512,64,128]{0,2,1:T(8,128)(2,1)} %bitcast.54, f32[512,64,128]{0,2,1:T(8,128)S(1)} %bitcast.56), kind=kLoop, calls=%fused_computation.17 | loop fusion | flops 8388608 | bytes 41943040 | tf_op jit(solution)/shard_map/mul | solution.py:68
  220.8 25.9 %all-gather.4.cloned.1.call-done = bf16[64,128,128]{2,1,0:T(8,128)(2,1)} async-done(((bf16[4,128,128]{2,1,0:T(8,128)(2,1)}), bf16[64,128,128]{2,1,0:T(8,128)(2,1)}) %all-gather.4.cloned.1.call-update) | async-done | bytes 2097168 | tf_op jit(solution)/shard_map/all_gather | solution.py:72
  246.7 16.9 %fusion.11 = f32[64,128,512]{2,1,0:T(8,128)} fusion(bf16[64,128,128]{2,1,0:T(8,128)(2,1)} %all-gather.4.cloned.1.call-done, f32[512,64,128]{0,2,1:T(8,128)} %bitcast_multiply_fusion), kind=kOutput, calls=%fused_computation.28 | convolution fusion | flops 6442450944 | bytes 35651584 | tf_op jit(solution)/shard_map/rbi,bij->rbj/dot_general | solution.py:79
  263.6 25.5 %all-gather.6.cloned.1.call-done = bf16[1,64,128,128]{3,2,0,1:T(8,128)(2,1)} async-done(((bf16[1,4,128,128]{3,2,0,1:T(8,128)(2,1)}), bf16[1,64,128,128]{3,2,0,1:T(8,128)(2,1)}) %all-gather.6.cloned.1.call-update) | async-done | bytes 2097168 | tf_op jit(solution)/shard_map/all_gather | solution.py:75
  289.1 16.9 %fusion.5 = f32[64,512,128]{1,2,0:T(8,128)} fusion(f32[64,128,512]{2,1,0:T(8,128)} %fusion.11, bf16[1,64,128,128]{3,2,0,1:T(8,128)(2,1)} %all-gather.6.cloned.1.call-done), kind=kOutput, calls=%fused_computation.15 | convolution fusion | flops 6442450944 | bytes 35651584 | tf_op jit(solution)/shard_map/rbi,bij->rbj/dot_general | solution.py:80
  306.0 12.5 %fusion.4 = bf16[1,512,8192]{1,2,0:T(8,128)(2,1)} fusion(f32[512,128]{0,1:T(8,128)S(1)} %copy.20, bf16[1,512,8192]{1,2,0:T(8,128)(2,1)} %copy.17, f32[1,512,8192]{1,2,0:T(8,128)} %bitcast.55), kind=kLoop, calls=%fused_computation.14 | loop fusion | flops 16777216 | bytes 33816576 | tf_op jit(solution)/shard_map/convert_element_type | solution.py:84
  318.5 11.9 %copy.30 = bf16[1,512,8192]{2,1,0:T(8,128)(2,1)} copy(bf16[1,512,8192]{1,2,0:T(8,128)(2,1)} %fusion.4) | data formatting | bytes 16777216
  (19 shorter events, 0.2 us)
Async XLA Ops:
  7.2 239.6 %all-gather.4.cloned.1.call-start = ((), (), s32[]{:S(2)}) async-start(), calls=%async_computation | async-start | bytes 2228224 | tf_op jit(solution)/shard_map/all_gather | solution.py:72
  7.2 12.0 %copy-start.2 = (s32[1,512,128]{2,1,0:T(8,128)S(1)}, s32[1,512,128]{2,1,0:T(8,128)}, u32[]{:S(2)}) copy-start(s32[1,512,128]{2,1,0:T(8,128)} %param.10) | copy-start | bytes 786436
  26.6 12.0 %copy-start = (f32[1,8192]{1,0:T(1,128)S(1)}, f32[1,8192]{1,0:T(1,128)}, u32[]{:S(2)}) copy-start(f32[1,8192]{1,0:T(1,128)} %param.8) | copy-start | bytes 98308
  38.6 168.6 %copy-start.3 = (f32[1,4,128,128]{3,2,1,0:T(8,128)S(1)}, f32[1,4,128,128]{3,2,1,0:T(8,128)}, u32[]{:S(2)}) copy-start(f32[1,4,128,128]{3,2,1,0:T(8,128)} %param.11) | copy-start | bytes 786436
  38.6 6.6 %collective-permute-start = (bf16[32,512]{1,0:T(8,128)(2,1)S(1)}, bf16[32,512]{1,0:T(8,128)(2,1)S(1)}, u32[]{:S(2)}, u32[]{:S(2)}) collective-permute-start(bf16[32,512]{1,0:T(8,128)(2,1)S(1)} %broadcast_select_fusion.2), channel_id=1, source_target_pairs={{0,16},{1,17},{2,18},{3,19},{4,20},{5,21},{6,22},{7,23},{8,24},{9,... | collective-permute-start | bytes 98312 | tf_op jit(solution)/shard_map/while/body/eval_jaxpr/ppermute | solution.py:13
  75.7 5.8 %collective-permute-start = (bf16[32,512]{1,0:T(8,128)(2,1)S(1)}, bf16[32,512]{1,0:T(8,128)(2,1)S(1)}, u32[]{:S(2)}, u32[]{:S(2)}) collective-permute-start(bf16[32,512]{1,0:T(8,128)(2,1)S(1)} %broadcast_select_fusion.2), channel_id=1, source_target_pairs={{0,16},{1,17},{2,18},{3,19},{4,20},{5,21},{6,22},{7,23},{8,24},{9,... | collective-permute-start | bytes 98312 | tf_op jit(solution)/shard_map/while/body/eval_jaxpr/ppermute | solution.py:13
  107.5 5.8 %collective-permute-start = (bf16[32,512]{1,0:T(8,128)(2,1)S(1)}, bf16[32,512]{1,0:T(8,128)(2,1)S(1)}, u32[]{:S(2)}, u32[]{:S(2)}) collective-permute-start(bf16[32,512]{1,0:T(8,128)(2,1)S(1)} %broadcast_select_fusion.2), channel_id=1, source_target_pairs={{0,16},{1,17},{2,18},{3,19},{4,20},{5,21},{6,22},{7,23},{8,24},{9,... | collective-permute-start | bytes 98312 | tf_op jit(solution)/shard_map/while/body/eval_jaxpr/ppermute | solution.py:13
  141.0 5.7 %collective-permute-start = (bf16[32,512]{1,0:T(8,128)(2,1)S(1)}, bf16[32,512]{1,0:T(8,128)(2,1)S(1)}, u32[]{:S(2)}, u32[]{:S(2)}) collective-permute-start(bf16[32,512]{1,0:T(8,128)(2,1)S(1)} %broadcast_select_fusion.2), channel_id=1, source_target_pairs={{0,16},{1,17},{2,18},{3,19},{4,20},{5,21},{6,22},{7,23},{8,24},{9,... | collective-permute-start | bytes 98312 | tf_op jit(solution)/shard_map/while/body/eval_jaxpr/ppermute | solution.py:13
  172.8 5.8 %collective-permute-start = (bf16[32,512]{1,0:T(8,128)(2,1)S(1)}, bf16[32,512]{1,0:T(8,128)(2,1)S(1)}, u32[]{:S(2)}, u32[]{:S(2)}) collective-permute-start(bf16[32,512]{1,0:T(8,128)(2,1)S(1)} %broadcast_select_fusion.2), channel_id=1, source_target_pairs={{0,16},{1,17},{2,18},{3,19},{4,20},{5,21},{6,22},{7,23},{8,24},{9,... | collective-permute-start | bytes 98312 | tf_op jit(solution)/shard_map/while/body/eval_jaxpr/ppermute | solution.py:13
  206.2 4.1 %copy-start.1 = (bf16[128,512]{1,0:T(8,128)(2,1)}, bf16[128,512]{1,0:T(8,128)(2,1)S(1)}, u32[]{:S(2)}) copy-start(bf16[128,512]{1,0:T(8,128)(2,1)S(1)} %get-tuple-element.224) | copy-start | bytes 393220
  207.1 82.0 %all-gather.6.cloned.1.call-start = ((), (), s32[]{:S(2)}) async-start(), calls=%async_computation.1 | async-start | bytes 2228224 | tf_op jit(solution)/shard_map/all_gather | solution.py:75
Sparse Core Ops, SparseCore 0:
  207.3 39.4 all-gather.3
  248.9 40.1 all-gather.5
where the time goes:
time: 339 us; the launch traced here: 337 us
  blocking collectives  102 us (30%)
  matrix products  64.5 us (19%)
  waiting for transfers between devices  59.3 us (17%)
  local copies, waits for them, and re-layouts  38.4 us (11%)
  other arithmetic  37.1 us (11%)
  starting transfers between devices  21.8 us (6%)
  between operations  14.2 us (4%)
    all_gather x5, blocking collectives, advance(): lax.all_gather(window, 'dp', axis=1, tiled=True).astype(jnp.float32)  102 us
    unnamed x11, local copies, waits for them, and re-layouts  35.9 us
    dot_general x5, matrix products, advance(): lax.dot_general(normed, kept_rows, (((1,), (1,)), ((), ())), preferred_el...  29.9 us
    all_gather x1, waiting for transfers between devices, body(): lax.all_gather(hessian_local.astype(jnp.bfloat16), 'dp', axis=0, tiled=True)  25.9 us
    all_gather x1, waiting for transfers between devices, body(): lax.all_gather(inverse_whole.astype(jnp.bfloat16), 'dp', axis=0, tiled=True)  25.5 us
    ppermute x5, starting transfers between devices, passed_along(): lax.ppermute(value, axis, [(source, source + steps) for source in range(f...  21.7 us
    dot_general x1, matrix products, body(): jnp.einsum('rbi,bij->rbj', gradient, inverse, precision=lax.Precision.HIG...  16.9 us
    dot_general x1, matrix products, body(): jnp.einsum('rbi,bij->rbj', removed, hessian, precision=lax.Precision.HIGH...  16.9 us
  transfers between devices with their start and end apart: 7, of which 7 were waited for; matrix products, arithmetic and copies ran while one was open for 9% of the time, Pallas kernels for 0%

commit v1 on v0

v1 whole, which is shorter than its diff:
```python
import functools

import jax
import jax.numpy as jnp
from jax import lax
from jax.experimental import pallas as pl
from jax.experimental.pallas import tpu as pltpu
from jax.sharding import PartitionSpec as P

BLOCK = 128
HALF = BLOCK // 2
VMEM_BYTES = 32 * 1024 * 1024


def keep_columns(masks_ref, cols):
    entries = masks_ref[0].astype(jnp.float32).astype(jnp.bfloat16)
    first = lax.broadcasted_iota(jnp.int32, (entries.shape[1], cols), 0) * HALF
    column = lax.broadcasted_iota(jnp.int32, (entries.shape[1], cols), 1) + pl.program_id(0) * cols
    spread = ((column >= first) & (column < first + HALF)).astype(jnp.float32).astype(jnp.bfloat16)
    return jnp.dot(entries, spread, preferred_element_type=jnp.float32)


def project_kernel(last, width, tokens, *refs):
    x_ref, gain_ref, weights_ref, masks_ref, window_ref, own_gain_ref, inverse_ref = refs[:7]
    out_ref = refs[7]
    total, squares = refs[-2:]
    step = pl.program_id(0)

    @pl.when(step == 0)
    def _():
        total[...] = jnp.zeros_like(total)
        squares[...] = jnp.zeros_like(squares)

    x = x_ref[0].astype(jnp.float32)
    squares[...] += jnp.sum(x * x, axis=1, keepdims=True)
    scaled = (x * gain_ref[...]).astype(jnp.bfloat16)
    kept = weights_ref[0] * keep_columns(masks_ref, x.shape[1]).astype(jnp.bfloat16)
    total[...] += lax.dot_general(
        scaled, kept, (((1,), (1,)), ((), ())), preferred_element_type=jnp.float32
    )

    @pl.when(step == pl.num_programs(0) - 1)
    def _():
        inverse_rms = lax.rsqrt(squares[...] * (1.0 / width) + 1e-05)
        window = window_ref[...].astype(jnp.float32)
        out_ref[...] = (window + total[...] * inverse_rms * width ** (-0.5)).astype(jnp.bfloat16)
        if last:
            factor_ref = refs[8]
            normed = (window * inverse_rms * own_gain_ref[...]).astype(jnp.bfloat16)
            for block in range(normed.shape[1] // BLOCK):
                columns = normed[:, block * BLOCK : (block + 1) * BLOCK]
                hessian = lax.dot_general(
                    columns, columns, (((0,), (0,)), ((), ())), preferred_element_type=jnp.float32
                ) * (1.0 / tokens)
                factor_ref[block] = jnp.dot(
                    hessian,
                    inverse_ref[0, block],
                    precision=lax.Precision.HIGHEST,
                    preferred_element_type=jnp.float32,
                ).astype(jnp.bfloat16)


def project(gathered, gains, weights, masks, window, own_gain, inv_hessian, last):
    steps, tokens, cols = gathered.shape
    _, rows, width = weights.shape
    whole = lambda shape: pl.BlockSpec(shape, lambda c: (0,) * len(shape))
    out_shape = [jax.ShapeDtypeStruct(window.shape, jnp.bfloat16)]
    if last:
        out_shape.append(jax.ShapeDtypeStruct(inv_hessian.shape[1:], jnp.bfloat16))
    return pl.pallas_call(
        functools.partial(project_kernel, last, width, tokens),
        grid=(steps,),
        in_specs=[
            pl.BlockSpec((1, tokens, cols), lambda c: (c, 0, 0)),
            pl.BlockSpec((1, cols), lambda c: (0, c)),
            pl.BlockSpec((1, rows, cols), lambda c: (0, 0, c)),
            whole(masks.shape),
            whole(window.shape),
            whole(own_gain.shape),
            whole(inv_hessian.shape),
        ],
        out_specs=[whole(s.shape) for s in out_shape],
        out_shape=out_shape,
        scratch_shapes=[
            pltpu.VMEM((tokens, rows), jnp.float32),
            pltpu.VMEM((tokens, 1), jnp.float32),
        ],
        compiler_params=pltpu.CompilerParams(vmem_limit_bytes=VMEM_BYTES),
        cost_estimate=pl.CostEstimate(
            flops=2 * tokens * rows * width, bytes_accessed=2 * rows * width, transcendentals=0
        ),
    )(gathered, gains, weights, masks, window, own_gain, inv_hessian)


def refit_kernel(weights_ref, masks_ref, factor_ref, out_ref):
    cols = weights_ref.shape[2]
    keep = keep_columns(masks_ref, cols)
    weights = weights_ref[0].astype(jnp.float32)
    removed = (weights * (1.0 - keep)).astype(jnp.bfloat16)
    for block in range(cols // BLOCK):
        part = slice(block * BLOCK, (block + 1) * BLOCK)
        update = jnp.dot(removed[:, part], factor_ref[0, block], preferred_element_type=jnp.float32)
        out_ref[0, :, part] = (keep[:, part] * (weights[:, part] + update)).astype(jnp.bfloat16)


def refit(weights, masks, factors):
    steps, blocks = factors.shape[:2]
    _, rows, width = weights.shape
    cols = blocks * BLOCK
    return pl.pallas_call(
        refit_kernel,
        grid=(steps,),
        in_specs=[
            pl.BlockSpec((1, rows, cols), lambda c: (0, 0, c)),
            pl.BlockSpec(masks.shape, lambda c: (0, 0, 0)),
            pl.BlockSpec((1, blocks, BLOCK, BLOCK), lambda c: (c, 0, 0, 0)),
        ],
        out_specs=pl.BlockSpec((1, rows, cols), lambda c: (0, 0, c)),
        out_shape=jax.ShapeDtypeStruct(weights.shape, jnp.bfloat16),
        compiler_params=pltpu.CompilerParams(vmem_limit_bytes=VMEM_BYTES),
        cost_estimate=pl.CostEstimate(
            flops=2 * rows * width * BLOCK, bytes_accessed=4 * rows * width, transcendentals=0
        ),
    )(weights, masks, factors)


def body(stream_in, gains, weights, masks, inv_hessian):
    section_index = lax.axis_index("section")
    sections = lax.axis_size("section")
    owned_cols = stream_in.shape[1]
    own_gain = lax.dynamic_slice_in_dim(gains, lax.axis_index("dp") * owned_cols, owned_cols, 1)
    window = stream_in
    for moment in range(sections):
        last = moment == sections - 1
        gathered = lax.all_gather(window, "dp")
        results = project(gathered, gains, weights, masks, window, own_gain, inv_hessian, last)
        if not last:
            received = lax.ppermute(
                results[0], "section", [(source, source + 1) for source in range(sections - 1)]
            )
            window = jnp.where(section_index == 0, stream_in, received)
    stream_out, factor = results
    refitted = refit(weights, masks, lax.all_gather(factor, "dp"))
    return stream_out[None], refitted


def solution(mesh):
    placed = (
        P(None, "dp"),
        P("section", None),
        P("section", "dp", None),
        P("section", "dp", None),
        P("section", "dp", None, None),
    )
    return jax.shard_map(
        body,
        mesh=mesh,
        in_specs=placed,
        out_specs=(P("section", None, "dp"), P("section", "dp", None)),
        check_vma=False,
    )
```

time: 339 us -> 201 us (0.59)
  blocking collectives: 102 us -> 0 us
  waiting for transfers between devices: 59.3 us -> 131 us
  matrix products: 64.5 us -> 0 us
  other arithmetic: 37.1 us -> 0.68 us
  Pallas kernels: 0 us -> 31.3 us
  starting transfers between devices: 21.8 us -> 3.5 us
  local copies, waits for them, and re-layouts: 38.4 us -> 20.1 us
    all_gather x5 -> x0, blocking collectives: 102 us -> none  [advance(): lax.all_gather(window, 'dp', axis=1, tiled=True).astype(jnp.float32)]
    all_gather x2 -> x3, waiting for transfers between devices: 51.4 us -> 127 us  [the longest x2 86.9 us: body(): gathered = lax.all_gather(window, 'dp')]
    dot_general x8 -> x0, matrix products: 64.5 us -> none  [the longest x5 29.9 us: advance(): lax.dot_general(normed, kept_rows, (((1,), (1,)), ((), ())), preferred_el...]
    pallas_call x0 -> x3, Pallas kernels: none -> 31.3 us  [the longest x2 20 us: project(): pl.pallas_call(functools.partial(project_kernel, last, width, tokens), gr...]
    ppermute x5 -> x1, starting transfers between devices: 21.7 us -> 3.38 us  [body(): lax.ppermute(results[0], 'section', [(source, source + 1) for source in r...]
    mul x2 -> x0, other arithmetic: 17.7 us -> none  [the longest x1 10.5 us: body(): removed = weights[0].astype(jnp.float32) * (1 - keep).astype(jnp.float32)]
    unnamed x11 -> x30, local copies, waits for them, and re-layouts: 35.9 us -> 19.4 us
    convert_element_type x8 -> x0, other arithmetic: 14.2 us -> none  [the longest x1 12.5 us: body(): return (produced[None], refitted.astype(jnp.bfloat16)[None])]
  transfers between devices with their start and end apart: 7 -> 4, of which waited for: 7 -> 4; matrix products, arithmetic and copies ran while one was open for 9% -> 0% of each run, Pallas kernels for 0% -> 0%
where the time goes in v1:
time: 201 us; the launch traced here: 200 us
  waiting for transfers between devices  131 us (65%)
  Pallas kernels  31.3 us (16%)
  local copies, waits for them, and re-layouts  20.1 us (10%)
  between operations  13.8 us (7%)
  starting transfers between devices  3.5 us (2%)
    all_gather x2, waiting for transfers between devices, body(): gathered = lax.all_gather(window, 'dp')  86.9 us
    all_gather x1, waiting for transfers between devices, body(): refitted = refit(weights, masks, lax.all_gather(factor, 'dp'))  40.3 us
    pallas_call x2, Pallas kernels, project(): pl.pallas_call(functools.partial(project_kernel, last, width, tokens), gr...  20 us
    unnamed x30, local copies, waits for them, and re-layouts  19.4 us
    pallas_call x1, Pallas kernels, refit(): pl.pallas_call(refit_kernel, grid=(steps,), in_specs=[pl.BlockSpec((1, ro...  11.2 us
  transfers between devices with their start and end apart: 4, of which 4 were waited for; matrix products, arithmetic and copies ran while one was open for 0% of the time, Pallas kernels for 0%

profile of v1, /device:TPU:0, one launch (start us, length us, event | category | flops | bytes accessed | tf_op | source)
XLA Modules:
  0.0 200.4 jit_solution(1499283173212238500)
XLA Ops:
  7.2 0.0 all-gather.7.cloned.1.call-start
  7.2 0.7 all-gather.7.cloned.1.call-update
  7.9 0.0 all-gather.9.cloned.1.call-start
  7.9 0.7 constant_dynamic-slice_fusion.refs_5_
  8.6 45.7 %all-gather.7.cloned.1.call-done = bf16[2048,512]{1,0:T(8,128)(2,1)} async-done(((bf16[128,512]{1,0:T(8,128)(2,1)}), bf16[2048,512]{1,0:T(8,128)(2,1)}) %all-gather.7.cloned.1.call-update) | async-done | bytes 2097168 | tf_op jit(solution)/shard_map/all_gather | solution.py:135
  54.3 0.0 copy-start
  54.3 3.4 %copy-done = bf16[1,512,8192]{2,1,0:T(8,128)(2,1)S(1)} copy-done((bf16[1,512,8192]{2,1,0:T(8,128)(2,1)S(1)}, bf16[1,512,8192]{2,1,0:T(8,128)(2,1)}, u32[]{:S(2)}) %copy-start) | copy-done | bytes 8388632
  57.7 0.0 copy-start.3
  57.7 0.9 copy-done.3
  58.6 0.0 copy-start.6
  58.6 1.6 copy-done.6
  60.2 0.0 copy-start.8
  60.2 0.9 copy-done.8
  61.1 0.0 copy-start.11
  61.1 0.9 copy-done.11
  62.1 0.0 copy-start.13
  62.1 0.8 copy-done.13
  62.8 0.0 copy-start.9
  62.8 0.0 copy-start.4
  62.8 0.0 copy-start.12
  62.8 0.0 copy-start.14
  62.8 9.3 %shard_map.68 = bf16[128,512]{1,0:T(8,128)(2,1)S(1)} custom-call(bf16[16,128,512]{2,1,0:T(8,128)(2,1)S(1)} %bitcast.5, f32[1,8192]{1,0:T(1,128)S(1)} %copy-done.13, bf16[1,512,8192]{2,1,0:T(8,128)(2,1)S(1)} %copy-done, s32[1,512,128]{2,1,0:T(8,128)S(1)} %copy-done.3, bf16[128,512]{1,0:T(8,128)(2,1)S(1)} %copy-done.8, ...), custom_call_target="tpu_custom_call" | custom-call | flops 1073741824 | bytes 8388608 | tf_op jit(solution)/shard_map/pallas_call | solution.py:70
  72.2 3.4 %collective-permute-start = (bf16[128,512]{1,0:T(8,128)(2,1)S(1)}, bf16[128,512]{1,0:T(8,128)(2,1)S(1)}, u32[]{:S(2)}, u32[]{:S(2)}) collective-permute-start(bf16[128,512]{1,0:T(8,128)(2,1)S(1)} %shard_map.68), channel_id=1, source_target_pairs={{0,16},{1,17},{2,18},{3,19},{4,20},{5,21},{6,22},{7,23},{8,24},{9,... | collective-permute-start | bytes 393224 | tf_op jit(solution)/shard_map/ppermute | solution.py:138
  75.6 3.1 %collective-permute-done = bf16[128,512]{1,0:T(8,128)(2,1)S(1)} collective-permute-done((bf16[128,512]{1,0:T(8,128)(2,1)S(1)}, bf16[128,512]{1,0:T(8,128)(2,1)S(1)}, u32[]{:S(2)}, u32[]{:S(2)}) %collective-permute-start) | collective-permute-done | bytes 131104 | tf_op jit(solution)/shard_map/ppermute | solution.py:138
  78.7 0.0 copy-done.9
  78.7 0.7 broadcast_select_fusion.refs_4_
  79.4 0.0 all-gather.9.cloned.1.call-update
  79.4 0.0 all-gather.11.cloned.1.call-start
  79.5 41.3 %all-gather.9.cloned.1.call-done = bf16[2048,512]{1,0:T(8,128)(2,1)} async-done(((bf16[128,512]{1,0:T(8,128)(2,1)}), bf16[2048,512]{1,0:T(8,128)(2,1)}) %all-gather.9.cloned.1.call-update) | async-done | bytes 2097168 | tf_op jit(solution)/shard_map/all_gather | solution.py:135
  120.7 0.0 copy-done.4
  120.7 0.0 copy-done.12
  120.7 0.0 copy-done.14
  120.7 0.0 copy-start.1
  120.8 3.4 %copy-done.1 = bf16[1,512,8192]{2,1,0:T(8,128)(2,1)S(1)} copy-done((bf16[1,512,8192]{2,1,0:T(8,128)(2,1)S(1)}, bf16[1,512,8192]{2,1,0:T(8,128)(2,1)}, u32[]{:S(2)}) %copy-start.1) | copy-done | bytes 8388632
  124.1 0.0 copy-start.7
  124.1 1.6 copy-done.7
  125.7 0.0 copy-start.10
  125.7 0.9 copy-done.10
  126.6 10.7 %shard_map.69 = (bf16[128,512]{1,0:T(8,128)(2,1)}, bf16[4,128,128]{2,1,0:T(8,128)(2,1)}) custom-call(bf16[16,128,512]{2,1,0:T(8,128)(2,1)S(1)} %bitcast.6, f32[1,8192]{1,0:T(1,128)S(1)} %copy-done.14, bf16[1,512,8192]{2,1,0:T(8,128)(2,1)S(1)} %copy-done.1, s32[1,512,128]{2,1,0:T(8,128)S(1)} %copy-done.4, bf16[128,512]{1,0:T(8,128)(2,1)S(1)} %copy-done.10, ...), custom_call_target="tpu_custom_call" | custom-call | flops 1073741824 | bytes 8388608 | tf_op jit(solution)/shard_map/pallas_call | solution.py:70
  137.4 0.0 all-gather.11.cloned.1.call-update
  137.4 40.3 %all-gather.11.cloned.1.call-done = bf16[64,128,128]{2,1,0:T(8,128)(2,1)} async-done(((bf16[4,128,128]{2,1,0:T(8,128)(2,1)}), bf16[64,128,128]{2,1,0:T(8,128)(2,1)}) %all-gather.11.cloned.1.call-update) | async-done | bytes 2097168 | tf_op jit(solution)/shard_map/all_gather | solution.py:143
  177.7 0.0 copy-start.2
  177.7 3.4 %copy-done.2 = bf16[1,512,8192]{2,1,0:T(8,128)(2,1)S(1)} copy-done((bf16[1,512,8192]{2,1,0:T(8,128)(2,1)S(1)}, bf16[1,512,8192]{2,1,0:T(8,128)(2,1)}, u32[]{:S(2)}) %copy-start.2) | copy-done | bytes 8388632
  181.1 0.0 copy-start.5
  181.1 1.6 copy-done.5
  182.7 11.2 %shard_map.70 = bf16[1,512,8192]{2,1,0:T(8,128)(2,1)} custom-call(bf16[1,512,8192]{2,1,0:T(8,128)(2,1)S(1)} %copy-done.2, s32[1,512,128]{2,1,0:T(8,128)S(1)} %copy-done.4, bf16[16,4,128,128]{3,2,1,0:T(8,128)(2,1)S(1)} %bitcast.4), custom_call_target="tpu_custom_call" | custom-call | flops 1073741824 | bytes 16777216 | tf_op jit(solution)/shard_map/pallas_call | solution.py:110
Async XLA Ops:
  7.2 47.1 %all-gather.7.cloned.1.call-start = ((), (), s32[]{:S(2)}) async-start(), calls=%async_computation | async-start | bytes 2228224 | tf_op jit(solution)/shard_map/all_gather | solution.py:135
  7.9 112.8 %all-gather.9.cloned.1.call-start = ((), (), s32[]{:S(2)}) async-start(), calls=%async_computation.1 | async-start | bytes 2228224 | tf_op jit(solution)/shard_map/all_gather | solution.py:135
  54.3 3.4 %copy-start = (bf16[1,512,8192]{2,1,0:T(8,128)(2,1)S(1)}, bf16[1,512,8192]{2,1,0:T(8,128)(2,1)}, u32[]{:S(2)}) copy-start(bf16[1,512,8192]{2,1,0:T(8,128)(2,1)} %weights_ref.1) | copy-start | bytes 25165828
  57.7 0.9 copy-start.3
  58.6 1.6 copy-start.6
  60.2 0.9 copy-start.8
  61.1 0.9 copy-start.11
  62.1 0.8 copy-start.13
  62.8 15.9 %copy-start.9 = (bf16[128,512]{1,0:T(8,128)(2,1)S(1)}, bf16[128,512]{1,0:T(8,128)(2,1)}, u32[]{:S(2)}) copy-start(bf16[128,512]{1,0:T(8,128)(2,1)} %refs_4_.1) | copy-start | bytes 393220
  62.8 57.9 %copy-start.4 = (s32[1,512,128]{2,1,0:T(8,128)S(1)}, s32[1,512,128]{2,1,0:T(8,128)}, u32[]{:S(2)}) copy-start(s32[1,512,128]{2,1,0:T(8,128)} %masks_ref.1) | copy-start | bytes 786436
  62.8 57.9 %copy-start.12 = (f32[1,4,128,128]{3,2,1,0:T(8,128)S(1)}, f32[1,4,128,128]{3,2,1,0:T(8,128)}, u32[]{:S(2)}) copy-start(f32[1,4,128,128]{3,2,1,0:T(8,128)} %refs_6_.3) | copy-start | bytes 786436
  62.8 57.9 %copy-start.14 = (f32[1,8192]{1,0:T(1,128)S(1)}, f32[1,8192]{1,0:T(1,128)}, u32[]{:S(2)}) copy-start(f32[1,8192]{1,0:T(1,128)} %refs_1_.3) | copy-start | bytes 98308
  72.2 6.5 %collective-permute-start = (bf16[128,512]{1,0:T(8,128)(2,1)S(1)}, bf16[128,512]{1,0:T(8,128)(2,1)S(1)}, u32[]{:S(2)}, u32[]{:S(2)}) collective-permute-start(bf16[128,512]{1,0:T(8,128)(2,1)S(1)} %shard_map.68), channel_id=1, source_target_pairs={{0,16},{1,17},{2,18},{3,19},{4,20},{5,21},{6,22},{7,23},{8,24},{9,... | collective-permute-start | bytes 393224 | tf_op jit(solution)/shard_map/ppermute | solution.py:138
  79.4 98.3 %all-gather.11.cloned.1.call-start = ((), (), s32[]{:S(2)}) async-start(), calls=%async_computation.2 | async-start | bytes 2228224 | tf_op jit(solution)/shard_map/all_gather | solution.py:143
  120.7 3.4 %copy-start.1 = (bf16[1,512,8192]{2,1,0:T(8,128)(2,1)S(1)}, bf16[1,512,8192]{2,1,0:T(8,128)(2,1)}, u32[]{:S(2)}) copy-start(bf16[1,512,8192]{2,1,0:T(8,128)(2,1)} %weights_ref.1) | copy-start | bytes 25165828
  124.1 1.6 copy-start.7
  125.7 0.9 copy-start.10
  177.7 3.4 %copy-start.2 = (bf16[1,512,8192]{2,1,0:T(8,128)(2,1)S(1)}, bf16[1,512,8192]{2,1,0:T(8,128)(2,1)}, u32[]{:S(2)}) copy-start(bf16[1,512,8192]{2,1,0:T(8,128)(2,1)} %weights_ref.1) | copy-start | bytes 25165828
  181.1 1.6 copy-start.5
Sparse Core Ops, SparseCore 0:
  10.2 44.0 all-gather.6
  79.5 41.1 all-gather.8
  137.5 40.1 all-gather.10
